TPU v7x, 32 devices: a whole 2x2x4 slice. The times are simulated.
32 devices in a mesh: dom: 8 (over z, y), sub: 4 (over x, core).
Axes of the slice: x: 2, y: 2, z: 4, core: 2. Of those that a mesh axis runs over, the one named last changes fastest.
Arguments:
- charges: float32 [4096, 256], P(('dom', 'sub')), may hold values from -0.3 to 0.3
- points: float32 [3, 4096, 256], P(None, ('dom', 'sub')), may hold values from -1 to 1
- leaf_basis: float32 [4096, 64, 256], P(('dom', 'sub')), may hold values from -0.375 to 0.375
- child_transfer: float32 [4096, 64, 64], P(('dom', 'sub')), may hold values from -0.75 to 0.75
- parent_transfer: float32 [512, 64, 64], P(('dom', 'sub')), may hold values from -0.75 to 0.75
- nodes_leaf: float32 [3, 4096, 64], P(None, ('dom', 'sub')), may hold values from -2 to 2
- nodes_mid: float32 [3, 512, 64], P(None, ('dom', 'sub')), may hold values from -2 to 2
- nodes_top: float32 [3, 64, 64], P(None, ('dom', 'sub')), may hold values from -2 to 2
- near_list: int32 [4096, 6], P(('dom', 'sub')), may hold values from -1 to 4095, as said below
- far_leaf: int32 [4096, 16], P(('dom', 'sub')), may hold values from -1 to 4095, as said below
- far_mid: int32 [512, 16], P(('dom', 'sub')), may hold values from -1 to 511, as said below
- far_top: int32 [64, 16], P(('dom', 'sub')), may hold values from -1 to 63, as said below
Outputs:
- potential: float32 [4096, 256], P(('dom', 'sub'))
Inputs may be any that keep to these rules, and one draw needn't show every extreme that they name: `near_list`: -1 marks an empty entry; a row's live entries come first, and its first entry is the leaf itself. Row l names only leaves of the aligned block of 128 leaves that holds l or of the blocks beside it. Some rows have all 6 entries live. `far_leaf`: -1 marks an empty entry; a row's live entries come first. Within each aligned block of 128 rows, the entries, empty ones counted, name clusters of each aligned block of 128 clusters exactly 64 times; in some row blocks all entries are live. `far_mid`: -1 marks an empty entry; a row's live entries come first. Within each aligned block of 16 rows, the entries, empty ones counted, name clusters of each aligned block of 16 clusters exactly 8 times; in some row blocks all entries are live. `far_top`: -1 marks an empty entry; a row's live entries come first; in some aligned blocks of 2 rows all entries are live.
All inputs are finite; a program needn't handle non-finite values.
Results may differ from a plain program's by a relative error of at most 0.0003.
Values sent between devices are 32-bit elements; how exact they have to be, the bound alone decides.
A program may use at most 64 MiB of HBM per device.

v0:
```python
import jax
import jax.numpy as jnp
from jax import lax
from jax.sharding import PartitionSpec as P

soften = 0.25
group_rows = 32


def with_halo(cells, sides, width):
    for axis, dim in sides:
        count = lax.axis_size(axis)
        ends = count - 1
        head = lax.slice_in_dim(cells, 0, width, axis=dim)
        tail = lax.slice_in_dim(cells, cells.shape[dim] - width, cells.shape[dim], axis=dim)
        cells = jnp.concatenate(
            [
                lax.ppermute(tail, axis, [(i, (i + 1) % count) for i in range(ends)]),
                cells,
                lax.ppermute(head, axis, [((i + 1) % count, i) for i in range(ends)]),
            ],
            axis=dim,
        )
    return cells


def kernel(delta_x, delta_y, delta_z):
    return lax.rsqrt(delta_x * delta_x + delta_y * delta_y + delta_z * delta_z + soften)


def near_field(targets, table, picks_all, validity):
    row_count = targets.shape[1]
    width = targets.shape[2]
    groups = row_count // group_rows
    weights_all = validity.astype(jnp.float32)

    def one_group(group):
        start = group * group_rows
        target = lax.dynamic_slice_in_dim(targets, start, group_rows, 1)
        picks = lax.dynamic_slice_in_dim(picks_all, start, group_rows, 0)
        weights = lax.dynamic_slice_in_dim(weights_all, start, group_rows, 0)

        def one_accumulate(column, running):
            chosen = lax.dynamic_index_in_dim(picks, column, 1, keepdims=False)
            weight = lax.dynamic_index_in_dim(weights, column, 1, keepdims=False)
            nearby = jnp.take(table, chosen, axis=0)
            values = kernel(
                target[0][:, :, None] - nearby[:, None, 0:width],
                target[1][:, :, None] - nearby[:, None, width : 2 * width],
                target[2][:, :, None] - nearby[:, None, 2 * width : 3 * width],
            )
            return (
                running + jnp.sum(values * nearby[:, None, 3 * width :], axis=2) * weight[:, None]
            )

        return lax.fori_loop(
            0, picks.shape[1], one_accumulate, jnp.zeros((group_rows, width), jnp.float32)
        )

    return lax.map(one_group, jnp.arange(groups, dtype=jnp.int32)).reshape(row_count, width)


def couple(own_nodes, remote, validity):
    rank_width = own_nodes.shape[2]

    def couple_accumulate(column, running):
        piece = lax.dynamic_index_in_dim(remote, column, 1, keepdims=False)
        weight = lax.dynamic_index_in_dim(validity, column, 1, keepdims=False)
        values = kernel(
            own_nodes[0][:, :, None] - piece[:, None, rank_width : 2 * rank_width],
            own_nodes[1][:, :, None] - piece[:, None, 2 * rank_width : 3 * rank_width],
            own_nodes[2][:, :, None] - piece[:, None, 3 * rank_width :],
        )
        return running + jnp.sum(values * piece[:, None, 0:rank_width], axis=2) * weight[:, None]

    return lax.fori_loop(
        0,
        remote.shape[1],
        couple_accumulate,
        jnp.zeros((own_nodes.shape[1], rank_width), jnp.float32),
    )


def make_table(moments, nodes):
    joined = jnp.concatenate([moments[:, None, :], jnp.transpose(nodes, (1, 0, 2))], axis=1)
    return joined.reshape(moments.shape[0], -1)


def split_ids(lists, per_shard):
    entries = lists.reshape(-1)
    validity = entries >= 0
    owners = jnp.where(validity, entries // per_shard, 0)
    wanted = jnp.where(validity, entries % per_shard, 0)
    return (owners, wanted, validity)


def fetch(table, owners, wanted, validity, capacity):
    shards = lax.axis_size(("dom", "sub"))
    hit_table = (
        (owners[:, None] == jnp.arange(shards, dtype=jnp.int32)[None, :]) & validity[:, None]
    ).astype(jnp.int32)
    rank_slot = jnp.sum((jnp.cumsum(hit_table, axis=0) - 1) * hit_table, axis=1)
    places = jnp.where(validity, owners * capacity + rank_slot, shards * capacity)
    requests = (
        jnp.zeros((shards * capacity,), jnp.int32)
        .at[places]
        .set(wanted, mode="drop")
        .reshape(shards, capacity)
    )
    replies = jnp.take(
        table,
        lax.all_to_all(requests, ("dom", "sub"), split_axis=0, concat_axis=0, tiled=True),
        axis=0,
    )
    answers = lax.all_to_all(replies, ("dom", "sub"), split_axis=0, concat_axis=0, tiled=True)
    flattened = answers.reshape(shards * capacity, table.shape[1])
    return jnp.take(flattened, jnp.minimum(places, shards * capacity - 1), axis=0)


def local(
    charges,
    points,
    leaf_basis,
    child_transfer,
    parent_transfer,
    nodes_leaf,
    nodes_mid,
    nodes_top,
    near_list,
    far_leaf,
    far_mid,
    far_top,
):
    highest = lax.Precision.HIGHEST
    shards = lax.axis_size(("dom", "sub"))
    leaf_count = charges.shape[0]
    mid_count = leaf_count // 8
    top_count = mid_count // 8
    rank_width = leaf_basis.shape[1]
    fan_out = far_leaf.shape[1]
    leaf_moments = jnp.einsum("lrp,lp->lr", leaf_basis, charges, precision=highest)
    mid_moments = (
        jnp.einsum("lij,lj->li", child_transfer, leaf_moments, precision=highest)
        .reshape(mid_count, 8, rank_width)
        .sum(axis=1)
    )
    top_moments = (
        jnp.einsum("lij,lj->li", parent_transfer, mid_moments, precision=highest)
        .reshape(top_count, 8, rank_width)
        .sum(axis=1)
    )
    leaf_table = make_table(leaf_moments, nodes_leaf)
    mid_table = make_table(mid_moments, nodes_mid)
    top_table = make_table(top_moments, nodes_top)
    leaf_owner, leaf_wanted, leaf_valid = split_ids(far_leaf, leaf_count)
    mid_owner, mid_wanted, mid_valid = split_ids(far_mid, mid_count)
    cap_leaf = leaf_count * fan_out // shards
    cap_mid = mid_count * fan_out // shards
    leaf_rows = fetch(leaf_table, leaf_owner, leaf_wanted, leaf_valid, cap_leaf)
    mid_rows = fetch(mid_table, mid_owner, mid_wanted, mid_valid, cap_mid)
    every_top = lax.all_gather(top_table, ("dom", "sub"), axis=0, tiled=True)
    top_rows = jnp.take(every_top, jnp.maximum(far_top.reshape(-1), 0), axis=0)
    leaf_local = couple(
        nodes_leaf,
        leaf_rows.reshape(leaf_count, fan_out, 4 * rank_width),
        leaf_valid.reshape(leaf_count, fan_out).astype(jnp.float32),
    )
    mid_local = couple(
        nodes_mid,
        mid_rows.reshape(mid_count, fan_out, 4 * rank_width),
        mid_valid.reshape(mid_count, fan_out).astype(jnp.float32),
    )
    top_local = couple(
        nodes_top,
        top_rows.reshape(top_count, fan_out, 4 * rank_width),
        (far_top >= 0).astype(jnp.float32),
    )
    mid_down = mid_local + jnp.einsum(
        "lji,lj->li", parent_transfer, jnp.repeat(top_local, 8, axis=0), precision=highest
    )
    leaf_down = leaf_local + jnp.einsum(
        "lji,lj->li", child_transfer, jnp.repeat(mid_down, 8, axis=0), precision=highest
    )
    position = lax.axis_index(("dom", "sub"))
    point_width = charges.shape[1]
    source_rows = jnp.concatenate(
        [jnp.transpose(points, (1, 0, 2)), charges[:, None, :]], axis=1
    ).reshape(leaf_count, 4 * point_width)
    widened = with_halo(source_rows, ((("dom", "sub"), 0),), leaf_count)
    near_valid = near_list >= 0
    near_picks = jnp.where(near_valid, near_list - (position - 1) * leaf_count, 0)
    near_sum = near_field(points, widened, near_picks, near_valid)
    return jnp.einsum("lrp,lr->lp", leaf_basis, leaf_down, precision=highest) + near_sum


def solution(mesh):
    placed = (
        P(("dom", "sub"), None),
        P(None, ("dom", "sub"), None),
        P(("dom", "sub"), None, None),
        P(("dom", "sub"), None, None),
        P(("dom", "sub"), None, None),
        P(None, ("dom", "sub"), None),
        P(None, ("dom", "sub"), None),
        P(None, ("dom", "sub"), None),
        P(("dom", "sub"), None),
        P(("dom", "sub"), None),
        P(("dom", "sub"), None),
        P(("dom", "sub"), None),
    )
    return jax.shard_map(
        local, mesh=mesh, in_specs=placed, out_specs=P(("dom", "sub"), None), check_vma=False
    )
```

profile of v0, /device:TPU:0, one launch (start us, length us, event | category | flops | bytes accessed | tf_op | source)
XLA Modules:
  0.0 343.3 jit_solution(582760452912788901)
XLA Ops:
  2.0 3.2 collective-permute-start
  9.8 8.4 %all-to-all-start.2 = ((s32[32,1,8]{2,1,0:T(1,128)}), s32[32,1,8]{2,1,0:T(1,128)S(1)}, u32[]{:S(2)}, u32[]{:S(2)}) async-start(s32[32,1,8]{2,1,0:T(1,128)} %bitcast.21), calls=%async_computation.2 | async-start | bytes 32768 | tf_op jit(solution)/shard_map/all_to_all | solution.py:112
  18.8 9.1 %reduce-window.14 = s32[32,16,128]{2,1,0:T(8,128)S(1)} reduce-window(s32[32,16,128]{2,1,0:T(8,128)S(1)} %fusion.4, s32[]{:T(128)} %constant.350.clone.1), window={size=1x1x128 pad=0_0x0_0x127_0}, to_apply=%region_0.0 | reduce-window | flops 8323072 | bytes 524292 | tf_op jit(solution)/shard_map/reduce-window
  29.0 9.7 %fusion.5 = f32[128,1,64]{2,1,0:T(1,128)S(1)} fusion(f32[128,64,256]{2,1,0:T(8,128)} %param.24, f32[128,256,1]{1,0,2:T(8,128)S(1)} %bitcast.187), kind=kOutput, calls=%fused_computation.63 | convolution fusion | flops 25165824 | bytes 8552448 | tf_op jit(solution)/shard_map/lrp,lp->lr/dot_general | solution.py:141
  40.5 41.9 %all-gather = f32[32,2,256]{2,1,0:T(2,128)S(1)} all-gather(f32[1,2,256]{2,1,0:T(2,128)S(1)} %reshape.658), channel_id=1, replica_groups=mesh['dom'=8,'sub'=4] {'dom','sub'}, dimensions={0}, use_global_device_ids=true | all-gather | bytes 67584 | tf_op jit(solution)/shard_map/all_gather | solution.py:161
  83.4 6.2 %while.70 = (s32[]{:T(128)}, f32[2,64]{1,0:T(2,128)S(1)}, f32[3,2,64]{2,1,0:T(2,128)S(1)}, f32[2,16,256]{2,0,1:T(2,128)S(1)}, f32[2,16]{0,1:T(8,128)S(1)}, /*index=5*/s32[]{:T(128)}, s32[]{:T(128)}) while((s32[]{:T(128)}, f32[2,64]{1,0:T(2,128)S(1)}, f32[3,2,64]{2,1,0:T(2,128)S(1)}, f32[2,16,256]{2,0,1:T(2,128)S(1)}, ...), condition=%wide.region_18.19_spmd.clone, body=%wide.region_16.18_spmd.clone.sunk | while | flops 90371 | bytes 17015 | solution.py:76
  90.2 8.0 %scatter_custom_fusion = s32[2048]{0:T(1024)S(1)} fusion(s32[2048]{0:T(1024)S(1)} %bitcast.206, s32[2048]{0:T(1024)S(1)} %get-tuple-element.651, s32[]{:T(128)} %constant.350.clone.1), kind=kCustom, calls=%fused_computation.156 | custom fusion | bytes 8196 | tf_op jit(solution)/shard_map/scatter | solution.py:107
  99.5 2.5 all-to-all-start
  103.9 5.2 %all-to-all-done = s32[32,1,64]{2,1,0:T(1,128)S(1)} async-done(((s32[32,1,64]{2,1,0:T(1,128)}), s32[32,1,64]{2,1,0:T(1,128)S(1)}, u32[]{:S(2)}, u32[]{:S(2)}) %all-to-all-start) | async-done | bytes 8224 | tf_op jit(solution)/shard_map/all_to_all | solution.py:112
  109.1 2.6 all-to-all-start.3
  111.8 8.6 %gather_fusion.1 = f32[2048,256]{1,0:T(8,128)} fusion(f32[128,256]{1,0:T(8,128)S(1)} %copy.120, s32[2048]{0:T(1024)S(1)} %broadcast_clamp_fusion.1), kind=kCustom, calls=%fused_computation.1 | custom fusion | bytes 4202496 | tf_op jit(solution)/shard_map/jit(_take)/gather | solution.py:110
  120.4 3.3 broadcast_select_fusion.2
  123.7 6.1 %all-to-all-start.1 = ((f32[32,64,256]{2,1,0:T(8,128)}), f32[32,64,256]{2,1,0:T(8,128)}, u32[]{:S(2)}, u32[]{:S(2)}) async-start(f32[32,64,256]{2,1,0:T(8,128)} %broadcast_select_fusion.2), calls=%async_computation.1 | async-start | bytes 4194304 | tf_op jit(solution)/shard_map/all_to_all | solution.py:115
  131.0 13.9 %while.69 = (s32[]{:T(128)}, f32[16,64]{1,0:T(8,128)S(1)}, f32[3,16,64]{2,1,0:T(8,128)S(1)}, f32[16,16,256]{2,0,1:T(8,128)S(1)}, f32[16,16]{0,1:T(8,128)S(1)}, /*index=5*/s32[]{:T(128)}, s32[]{:T(128)}) while((s32[]{:T(128)}, f32[16,64]{1,0:T(8,128)S(1)}, f32[3,16,64]{2,1,0:T(8,128)S(1)}, f32[16,16,256]{2,0,1:T(8,128)S(1)}, ...), condition=%wide.region_14.15_spmd.clone, body=%wide.region_12.14_spmd.clone.sunk | while | flops 722947 | bytes 135455 | solution.py:76
  146.7 157.7 %while.67 = (s32[]{:T(128)}, f32[4,32,256]{2,1,0:T(8,128)S(1)}, s32[4]{0:T(128)S(1)}, s32[128,6]{0,1:T(8,128)S(1)}, f32[128,6]{0,1:T(8,128)S(1)}, /*index=5*/f32...) while((s32[]{:T(128)}, f32[4,32,256]{2,1,0:T(8,128)S(1)}, ...), condition=%wide.region_23.24_spmd, body=%wide.region_19.23_spmd.sunk | while | flops 23119044 | bytes 1614134 | solution.py:60
  149.0 37.1 %while.71 = (s32[]{:T(128)}, f32[32,256]{1,0:T(8,128)S(1)}, f32[3,32,256]{2,1,0:T(8,128)S(1)}, s32[32,6]{0,1:T(8,128)S(1)}, f32[384,1024]{1,0:T(8,128)S(1)}, /*index=5*/f32[32,6]{0,1:T(8,128)S(1)}, s32[]{:T(128)}, s32[]{:T(128)}) while((s32[]{:T(128)}, f32[32,256]{1,0:T(8,128)S(1)}, f32[3,32,256]{2,1,0:T(8,128)S(1)}, ...), condition=%wide.region_22.22_spmd.clone, body=%wide.region_20.21_spmd.clone.sunk | while | flops 23119040 | bytes 1348647 | solution.py:56
  149.8 5.3 %multiply_reduce_fusion.13 = f32[32,256]{1,0:T(8,128)S(1)} fusion(f32[32,256]{1,0:T(8,128)S(1)} %get-tuple-element.898, f32[32,256]{1,0:T(8,128)S(1)} %get-tuple-element.899, f32[32,256]{1,0:T(8,128)S(1)} %get-tuple-element.900, f32[32,256]{1,0:T(8,128)S(1)} %get-tuple-element.901, f32[32,256]{1,0:T(8,128)S(1)} %get-tuple-element.902, ...), kind=kLoop, calls=%fused_computation.8.clone.1 | loop fusion | flops 23060480 | bytes 262144 | tf_op jit(solution)/shard_map/while/body/eval_jaxpr/while/body/eval_jaxpr/reduce_sum | solution.py:53
  156.0 5.3 %multiply_reduce_fusion.13 = f32[32,256]{1,0:T(8,128)S(1)} fusion(f32[32,256]{1,0:T(8,128)S(1)} %get-tuple-element.898, f32[32,256]{1,0:T(8,128)S(1)} %get-tuple-element.899, f32[32,256]{1,0:T(8,128)S(1)} %get-tuple-element.900, f32[32,256]{1,0:T(8,128)S(1)} %get-tuple-element.901, f32[32,256]{1,0:T(8,128)S(1)} %get-tuple-element.902, ...), kind=kLoop, calls=%fused_computation.8.clone.1 | loop fusion | flops 23060480 | bytes 262144 | tf_op jit(solution)/shard_map/while/body/eval_jaxpr/while/body/eval_jaxpr/reduce_sum | solution.py:53
  162.2 5.3 %multiply_reduce_fusion.13 = f32[32,256]{1,0:T(8,128)S(1)} fusion(f32[32,256]{1,0:T(8,128)S(1)} %get-tuple-element.898, f32[32,256]{1,0:T(8,128)S(1)} %get-tuple-element.899, f32[32,256]{1,0:T(8,128)S(1)} %get-tuple-element.900, f32[32,256]{1,0:T(8,128)S(1)} %get-tuple-element.901, f32[32,256]{1,0:T(8,128)S(1)} %get-tuple-element.902, ...), kind=kLoop, calls=%fused_computation.8.clone.1 | loop fusion | flops 23060480 | bytes 262144 | tf_op jit(solution)/shard_map/while/body/eval_jaxpr/while/body/eval_jaxpr/reduce_sum | solution.py:53
  168.3 5.3 %multiply_reduce_fusion.13 = f32[32,256]{1,0:T(8,128)S(1)} fusion(f32[32,256]{1,0:T(8,128)S(1)} %get-tuple-element.898, f32[32,256]{1,0:T(8,128)S(1)} %get-tuple-element.899, f32[32,256]{1,0:T(8,128)S(1)} %get-tuple-element.900, f32[32,256]{1,0:T(8,128)S(1)} %get-tuple-element.901, f32[32,256]{1,0:T(8,128)S(1)} %get-tuple-element.902, ...), kind=kLoop, calls=%fused_computation.8.clone.1 | loop fusion | flops 23060480 | bytes 262144 | tf_op jit(solution)/shard_map/while/body/eval_jaxpr/while/body/eval_jaxpr/reduce_sum | solution.py:53
  174.5 5.3 %multiply_reduce_fusion.13 = f32[32,256]{1,0:T(8,128)S(1)} fusion(f32[32,256]{1,0:T(8,128)S(1)} %get-tuple-element.898, f32[32,256]{1,0:T(8,128)S(1)} %get-tuple-element.899, f32[32,256]{1,0:T(8,128)S(1)} %get-tuple-element.900, f32[32,256]{1,0:T(8,128)S(1)} %get-tuple-element.901, f32[32,256]{1,0:T(8,128)S(1)} %get-tuple-element.902, ...), kind=kLoop, calls=%fused_computation.8.clone.1 | loop fusion | flops 23060480 | bytes 262144 | tf_op jit(solution)/shard_map/while/body/eval_jaxpr/while/body/eval_jaxpr/reduce_sum | solution.py:53
  180.7 5.3 %multiply_reduce_fusion.13 = f32[32,256]{1,0:T(8,128)S(1)} fusion(f32[32,256]{1,0:T(8,128)S(1)} %get-tuple-element.898, f32[32,256]{1,0:T(8,128)S(1)} %get-tuple-element.899, f32[32,256]{1,0:T(8,128)S(1)} %get-tuple-element.900, f32[32,256]{1,0:T(8,128)S(1)} %get-tuple-element.901, f32[32,256]{1,0:T(8,128)S(1)} %get-tuple-element.902, ...), kind=kLoop, calls=%fused_computation.8.clone.1 | loop fusion | flops 23060480 | bytes 262144 | tf_op jit(solution)/shard_map/while/body/eval_jaxpr/while/body/eval_jaxpr/reduce_sum | solution.py:53
  188.5 37.1 %while.71 = (s32[]{:T(128)}, f32[32,256]{1,0:T(8,128)S(1)}, f32[3,32,256]{2,1,0:T(8,128)S(1)}, s32[32,6]{0,1:T(8,128)S(1)}, f32[384,1024]{1,0:T(8,128)S(1)}, /*index=5*/f32[32,6]{0,1:T(8,128)S(1)}, s32[]{:T(128)}, s32[]{:T(128)}) while((s32[]{:T(128)}, f32[32,256]{1,0:T(8,128)S(1)}, f32[3,32,256]{2,1,0:T(8,128)S(1)}, ...), condition=%wide.region_22.22_spmd.clone, body=%wide.region_20.21_spmd.clone.sunk | while | flops 23119040 | bytes 1348647 | solution.py:56
  189.2 5.3 %multiply_reduce_fusion.13 = f32[32,256]{1,0:T(8,128)S(1)} fusion(f32[32,256]{1,0:T(8,128)S(1)} %get-tuple-element.898, f32[32,256]{1,0:T(8,128)S(1)} %get-tuple-element.899, f32[32,256]{1,0:T(8,128)S(1)} %get-tuple-element.900, f32[32,256]{1,0:T(8,128)S(1)} %get-tuple-element.901, f32[32,256]{1,0:T(8,128)S(1)} %get-tuple-element.902, ...), kind=kLoop, calls=%fused_computation.8.clone.1 | loop fusion | flops 23060480 | bytes 262144 | tf_op jit(solution)/shard_map/while/body/eval_jaxpr/while/body/eval_jaxpr/reduce_sum | solution.py:53
  195.4 5.3 %multiply_reduce_fusion.13 = f32[32,256]{1,0:T(8,128)S(1)} fusion(f32[32,256]{1,0:T(8,128)S(1)} %get-tuple-element.898, f32[32,256]{1,0:T(8,128)S(1)} %get-tuple-element.899, f32[32,256]{1,0:T(8,128)S(1)} %get-tuple-element.900, f32[32,256]{1,0:T(8,128)S(1)} %get-tuple-element.901, f32[32,256]{1,0:T(8,128)S(1)} %get-tuple-element.902, ...), kind=kLoop, calls=%fused_computation.8.clone.1 | loop fusion | flops 23060480 | bytes 262144 | tf_op jit(solution)/shard_map/while/body/eval_jaxpr/while/body/eval_jaxpr/reduce_sum | solution.py:53
  201.6 5.3 %multiply_reduce_fusion.13 = f32[32,256]{1,0:T(8,128)S(1)} fusion(f32[32,256]{1,0:T(8,128)S(1)} %get-tuple-element.898, f32[32,256]{1,0:T(8,128)S(1)} %get-tuple-element.899, f32[32,256]{1,0:T(8,128)S(1)} %get-tuple-element.900, f32[32,256]{1,0:T(8,128)S(1)} %get-tuple-element.901, f32[32,256]{1,0:T(8,128)S(1)} %get-tuple-element.902, ...), kind=kLoop, calls=%fused_computation.8.clone.1 | loop fusion | flops 23060480 | bytes 262144 | tf_op jit(solution)/shard_map/while/body/eval_jaxpr/while/body/eval_jaxpr/reduce_sum | solution.py:53
  207.8 5.3 %multiply_reduce_fusion.13 = f32[32,256]{1,0:T(8,128)S(1)} fusion(f32[32,256]{1,0:T(8,128)S(1)} %get-tuple-element.898, f32[32,256]{1,0:T(8,128)S(1)} %get-tuple-element.899, f32[32,256]{1,0:T(8,128)S(1)} %get-tuple-element.900, f32[32,256]{1,0:T(8,128)S(1)} %get-tuple-element.901, f32[32,256]{1,0:T(8,128)S(1)} %get-tuple-element.902, ...), kind=kLoop, calls=%fused_computation.8.clone.1 | loop fusion | flops 23060480 | bytes 262144 | tf_op jit(solution)/shard_map/while/body/eval_jaxpr/while/body/eval_jaxpr/reduce_sum | solution.py:53
  214.0 5.3 %multiply_reduce_fusion.13 = f32[32,256]{1,0:T(8,128)S(1)} fusion(f32[32,256]{1,0:T(8,128)S(1)} %get-tuple-element.898, f32[32,256]{1,0:T(8,128)S(1)} %get-tuple-element.899, f32[32,256]{1,0:T(8,128)S(1)} %get-tuple-element.900, f32[32,256]{1,0:T(8,128)S(1)} %get-tuple-element.901, f32[32,256]{1,0:T(8,128)S(1)} %get-tuple-element.902, ...), kind=kLoop, calls=%fused_computation.8.clone.1 | loop fusion | flops 23060480 | bytes 262144 | tf_op jit(solution)/shard_map/while/body/eval_jaxpr/while/body/eval_jaxpr/reduce_sum | solution.py:53
  220.1 5.3 %multiply_reduce_fusion.13 = f32[32,256]{1,0:T(8,128)S(1)} fusion(f32[32,256]{1,0:T(8,128)S(1)} %get-tuple-element.898, f32[32,256]{1,0:T(8,128)S(1)} %get-tuple-element.899, f32[32,256]{1,0:T(8,128)S(1)} %get-tuple-element.900, f32[32,256]{1,0:T(8,128)S(1)} %get-tuple-element.901, f32[32,256]{1,0:T(8,128)S(1)} %get-tuple-element.902, ...), kind=kLoop, calls=%fused_computation.8.clone.1 | loop fusion | flops 23060480 | bytes 262144 | tf_op jit(solution)/shard_map/while/body/eval_jaxpr/while/body/eval_jaxpr/reduce_sum | solution.py:53
  227.9 37.1 %while.71 = (s32[]{:T(128)}, f32[32,256]{1,0:T(8,128)S(1)}, f32[3,32,256]{2,1,0:T(8,128)S(1)}, s32[32,6]{0,1:T(8,128)S(1)}, f32[384,1024]{1,0:T(8,128)S(1)}, /*index=5*/f32[32,6]{0,1:T(8,128)S(1)}, s32[]{:T(128)}, s32[]{:T(128)}) while((s32[]{:T(128)}, f32[32,256]{1,0:T(8,128)S(1)}, f32[3,32,256]{2,1,0:T(8,128)S(1)}, ...), condition=%wide.region_22.22_spmd.clone, body=%wide.region_20.21_spmd.clone.sunk | while | flops 23119040 | bytes 1348647 | solution.py:56
  228.6 5.3 %multiply_reduce_fusion.13 = f32[32,256]{1,0:T(8,128)S(1)} fusion(f32[32,256]{1,0:T(8,128)S(1)} %get-tuple-element.898, f32[32,256]{1,0:T(8,128)S(1)} %get-tuple-element.899, f32[32,256]{1,0:T(8,128)S(1)} %get-tuple-element.900, f32[32,256]{1,0:T(8,128)S(1)} %get-tuple-element.901, f32[32,256]{1,0:T(8,128)S(1)} %get-tuple-element.902, ...), kind=kLoop, calls=%fused_computation.8.clone.1 | loop fusion | flops 23060480 | bytes 262144 | tf_op jit(solution)/shard_map/while/body/eval_jaxpr/while/body/eval_jaxpr/reduce_sum | solution.py:53
  234.8 5.3 %multiply_reduce_fusion.13 = f32[32,256]{1,0:T(8,128)S(1)} fusion(f32[32,256]{1,0:T(8,128)S(1)} %get-tuple-element.898, f32[32,256]{1,0:T(8,128)S(1)} %get-tuple-element.899, f32[32,256]{1,0:T(8,128)S(1)} %get-tuple-element.900, f32[32,256]{1,0:T(8,128)S(1)} %get-tuple-element.901, f32[32,256]{1,0:T(8,128)S(1)} %get-tuple-element.902, ...), kind=kLoop, calls=%fused_computation.8.clone.1 | loop fusion | flops 23060480 | bytes 262144 | tf_op jit(solution)/shard_map/while/body/eval_jaxpr/while/body/eval_jaxpr/reduce_sum | solution.py:53
  241.0 5.3 %multiply_reduce_fusion.13 = f32[32,256]{1,0:T(8,128)S(1)} fusion(f32[32,256]{1,0:T(8,128)S(1)} %get-tuple-element.898, f32[32,256]{1,0:T(8,128)S(1)} %get-tuple-element.899, f32[32,256]{1,0:T(8,128)S(1)} %get-tuple-element.900, f32[32,256]{1,0:T(8,128)S(1)} %get-tuple-element.901, f32[32,256]{1,0:T(8,128)S(1)} %get-tuple-element.902, ...), kind=kLoop, calls=%fused_computation.8.clone.1 | loop fusion | flops 23060480 | bytes 262144 | tf_op jit(solution)/shard_map/while/body/eval_jaxpr/while/body/eval_jaxpr/reduce_sum | solution.py:53
  247.2 5.3 %multiply_reduce_fusion.13 = f32[32,256]{1,0:T(8,128)S(1)} fusion(f32[32,256]{1,0:T(8,128)S(1)} %get-tuple-element.898, f32[32,256]{1,0:T(8,128)S(1)} %get-tuple-element.899, f32[32,256]{1,0:T(8,128)S(1)} %get-tuple-element.900, f32[32,256]{1,0:T(8,128)S(1)} %get-tuple-element.901, f32[32,256]{1,0:T(8,128)S(1)} %get-tuple-element.902, ...), kind=kLoop, calls=%fused_computation.8.clone.1 | loop fusion | flops 23060480 | bytes 262144 | tf_op jit(solution)/shard_map/while/body/eval_jaxpr/while/body/eval_jaxpr/reduce_sum | solution.py:53
  253.4 5.3 %multiply_reduce_fusion.13 = f32[32,256]{1,0:T(8,128)S(1)} fusion(f32[32,256]{1,0:T(8,128)S(1)} %get-tuple-element.898, f32[32,256]{1,0:T(8,128)S(1)} %get-tuple-element.899, f32[32,256]{1,0:T(8,128)S(1)} %get-tuple-element.900, f32[32,256]{1,0:T(8,128)S(1)} %get-tuple-element.901, f32[32,256]{1,0:T(8,128)S(1)} %get-tuple-element.902, ...), kind=kLoop, calls=%fused_computation.8.clone.1 | loop fusion | flops 23060480 | bytes 262144 | tf_op jit(solution)/shard_map/while/body/eval_jaxpr/while/body/eval_jaxpr/reduce_sum | solution.py:53
  259.6 5.3 %multiply_reduce_fusion.13 = f32[32,256]{1,0:T(8,128)S(1)} fusion(f32[32,256]{1,0:T(8,128)S(1)} %get-tuple-element.898, f32[32,256]{1,0:T(8,128)S(1)} %get-tuple-element.899, f32[32,256]{1,0:T(8,128)S(1)} %get-tuple-element.900, f32[32,256]{1,0:T(8,128)S(1)} %get-tuple-element.901, f32[32,256]{1,0:T(8,128)S(1)} %get-tuple-element.902, ...), kind=kLoop, calls=%fused_computation.8.clone.1 | loop fusion | flops 23060480 | bytes 262144 | tf_op jit(solution)/shard_map/while/body/eval_jaxpr/while/body/eval_jaxpr/reduce_sum | solution.py:53
  267.3 37.1 %while.71 = (s32[]{:T(128)}, f32[32,256]{1,0:T(8,128)S(1)}, f32[3,32,256]{2,1,0:T(8,128)S(1)}, s32[32,6]{0,1:T(8,128)S(1)}, f32[384,1024]{1,0:T(8,128)S(1)}, /*index=5*/f32[32,6]{0,1:T(8,128)S(1)}, s32[]{:T(128)}, s32[]{:T(128)}) while((s32[]{:T(128)}, f32[32,256]{1,0:T(8,128)S(1)}, f32[3,32,256]{2,1,0:T(8,128)S(1)}, ...), condition=%wide.region_22.22_spmd.clone, body=%wide.region_20.21_spmd.clone.sunk | while | flops 23119040 | bytes 1348647 | solution.py:56
  268.1 5.3 %multiply_reduce_fusion.13 = f32[32,256]{1,0:T(8,128)S(1)} fusion(f32[32,256]{1,0:T(8,128)S(1)} %get-tuple-element.898, f32[32,256]{1,0:T(8,128)S(1)} %get-tuple-element.899, f32[32,256]{1,0:T(8,128)S(1)} %get-tuple-element.900, f32[32,256]{1,0:T(8,128)S(1)} %get-tuple-element.901, f32[32,256]{1,0:T(8,128)S(1)} %get-tuple-element.902, ...), kind=kLoop, calls=%fused_computation.8.clone.1 | loop fusion | flops 23060480 | bytes 262144 | tf_op jit(solution)/shard_map/while/body/eval_jaxpr/while/body/eval_jaxpr/reduce_sum | solution.py:53
  274.3 5.3 %multiply_reduce_fusion.13 = f32[32,256]{1,0:T(8,128)S(1)} fusion(f32[32,256]{1,0:T(8,128)S(1)} %get-tuple-element.898, f32[32,256]{1,0:T(8,128)S(1)} %get-tuple-element.899, f32[32,256]{1,0:T(8,128)S(1)} %get-tuple-element.900, f32[32,256]{1,0:T(8,128)S(1)} %get-tuple-element.901, f32[32,256]{1,0:T(8,128)S(1)} %get-tuple-element.902, ...), kind=kLoop, calls=%fused_computation.8.clone.1 | loop fusion | flops 23060480 | bytes 262144 | tf_op jit(solution)/shard_map/while/body/eval_jaxpr/while/body/eval_jaxpr/reduce_sum | solution.py:53
  280.4 5.3 %multiply_reduce_fusion.13 = f32[32,256]{1,0:T(8,128)S(1)} fusion(f32[32,256]{1,0:T(8,128)S(1)} %get-tuple-element.898, f32[32,256]{1,0:T(8,128)S(1)} %get-tuple-element.899, f32[32,256]{1,0:T(8,128)S(1)} %get-tuple-element.900, f32[32,256]{1,0:T(8,128)S(1)} %get-tuple-element.901, f32[32,256]{1,0:T(8,128)S(1)} %get-tuple-element.902, ...), kind=kLoop, calls=%fused_computation.8.clone.1 | loop fusion | flops 23060480 | bytes 262144 | tf_op jit(solution)/shard_map/while/body/eval_jaxpr/while/body/eval_jaxpr/reduce_sum | solution.py:53
  286.6 5.3 %multiply_reduce_fusion.13 = f32[32,256]{1,0:T(8,128)S(1)} fusion(f32[32,256]{1,0:T(8,128)S(1)} %get-tuple-element.898, f32[32,256]{1,0:T(8,128)S(1)} %get-tuple-element.899, f32[32,256]{1,0:T(8,128)S(1)} %get-tuple-element.900, f32[32,256]{1,0:T(8,128)S(1)} %get-tuple-element.901, f32[32,256]{1,0:T(8,128)S(1)} %get-tuple-element.902, ...), kind=kLoop, calls=%fused_computation.8.clone.1 | loop fusion | flops 23060480 | bytes 262144 | tf_op jit(solution)/shard_map/while/body/eval_jaxpr/while/body/eval_jaxpr/reduce_sum | solution.py:53
  292.8 5.3 %multiply_reduce_fusion.13 = f32[32,256]{1,0:T(8,128)S(1)} fusion(f32[32,256]{1,0:T(8,128)S(1)} %get-tuple-element.898, f32[32,256]{1,0:T(8,128)S(1)} %get-tuple-element.899, f32[32,256]{1,0:T(8,128)S(1)} %get-tuple-element.900, f32[32,256]{1,0:T(8,128)S(1)} %get-tuple-element.901, f32[32,256]{1,0:T(8,128)S(1)} %get-tuple-element.902, ...), kind=kLoop, calls=%fused_computation.8.clone.1 | loop fusion | flops 23060480 | bytes 262144 | tf_op jit(solution)/shard_map/while/body/eval_jaxpr/while/body/eval_jaxpr/reduce_sum | solution.py:53
  299.0 5.3 %multiply_reduce_fusion.13 = f32[32,256]{1,0:T(8,128)S(1)} fusion(f32[32,256]{1,0:T(8,128)S(1)} %get-tuple-element.898, f32[32,256]{1,0:T(8,128)S(1)} %get-tuple-element.899, f32[32,256]{1,0:T(8,128)S(1)} %get-tuple-element.900, f32[32,256]{1,0:T(8,128)S(1)} %get-tuple-element.901, f32[32,256]{1,0:T(8,128)S(1)} %get-tuple-element.902, ...), kind=kLoop, calls=%fused_computation.8.clone.1 | loop fusion | flops 23060480 | bytes 262144 | tf_op jit(solution)/shard_map/while/body/eval_jaxpr/while/body/eval_jaxpr/reduce_sum | solution.py:53
  304.4 8.2 %gather_fusion.2 = f32[2048,256]{1,0:T(8,128)S(1)} fusion(f32[2048,256]{1,0:T(8,128)} %bitcast.15, s32[2048]{0:T(1024)S(1)} %broadcast_clamp_fusion), kind=kCustom, calls=%fused_computation.2 | custom fusion | bytes 4202496 | tf_op jit(solution)/shard_map/jit(_take)/gather | solution.py:117
  312.7 1.9 copy.121
  314.6 1.8 broadcast_select_fusion.1
  316.4 19.7 %while.68 = (s32[]{:T(128)}, f32[128,64]{0,1:T(8,128)S(1)}, f32[3,128,64]{1,2,0:T(8,128)S(1)}, f32[128,16,256]{0,2,1:T(8,128)S(1)}, f32[128,16]{0,1:T(8,128)S(1)}, /*index=5*/s32[]{:T(128)}, s32[]{:T(128)}) while((s32[]{:T(128)}, f32[128,64]{0,1:T(8,128)S(1)}, f32[3,128,64]{1,2,0:T(8,128)S(1)}, f32[128,16,256]{0,2,1:T(8,128)S(1)}, ...), condition=%wide.region_6.7_spmd.clone, body=%wide.region_4.6_spmd.clone.sunk | while | flops 5783555 | bytes 1082975 | solution.py:76
  336.2 6.4 %fusion.53 = f32[128,1,256]{2,1,0:T(1,128)S(1)} fusion(f32[128,64,1]{1,2,0:T(1,128)S(1)} %copy.151, f32[128,64,256]{2,1,0:T(8,128)} %param.24), kind=kOutput, calls=%fused_computation.196 | convolution fusion | flops 25165824 | bytes 8552448 | tf_op jit(solution)/shard_map/lrp,lr->lp/dot_general | solution.py:193
  (630 shorter events, 82.6 us)
Async XLA Ops:
  0.0 39.4 %copy-start = (f32[16,64,64]{2,1,0:T(8,128)S(1)}, f32[16,64,64]{2,1,0:T(8,128)}, u32[]{:S(2)}) copy-start(f32[16,64,64]{2,1,0:T(8,128)} %param.26) | copy-start | bytes 786436
  0.0 6.5 %copy-start.6 = (s32[16,16]{1,0:T(8,128)S(1)}, s32[16,16]{1,0:T(8,128)}, u32[]{:S(2)}) copy-start(s32[16,16]{1,0:T(8,128)} %param.32) | copy-start | bytes 3076
  0.0 18.3 %copy-start.9 = (s32[128,16]{0,1:T(8,128)S(1)}, s32[128,16]{0,1:T(8,128)}, u32[]{:S(2)}) copy-start(s32[128,16]{0,1:T(8,128)} %param.31) | copy-start | bytes 24580
  0.0 18.8 %copy-start.10 = (s32[2,16]{1,0:T(2,128)S(1)}, s32[2,16]{1,0:T(2,128)}, u32[]{:S(2)}) copy-start(s32[2,16]{1,0:T(2,128)} %param.33) | copy-start | bytes 388
  1.2 27.8 %copy-start.4 = (f32[128,256]{1,0:T(8,128)S(1)}, f32[128,256]{1,0:T(8,128)}, u32[]{:S(2)}) copy-start(f32[128,256]{1,0:T(8,128)} %param.22) | copy-start | bytes 393220
  2.0 143.2 %collective-permute-start = (f32[128,1024]{1,0:T(8,128)}, f32[128,1024]{1,0:T(8,128)}, u32[]{:S(2)}, u32[]{:S(2)}) collective-permute-start(f32[128,1024]{1,0:T(8,128)} %bitcast.79), channel_id=1, source_target_pairs={{0,1},{1,2},{2,3},{3,4},{4,5},{5,6},{6,7},{7,8},{8,9},{9,10},{10,1... | collective-permute-start | bytes 1572872 | tf_op jit(solution)/shard_map/ppermute | solution.py:18
  5.2 140.0 %collective-permute-start.1 = (f32[128,1024]{1,0:T(8,128)}, f32[128,1024]{1,0:T(8,128)}, u32[]{:S(2)}, u32[]{:S(2)}) collective-permute-start(f32[128,1024]{1,0:T(8,128)} %bitcast.79), channel_id=1, source_target_pairs={{1,0},{2,1},{3,2},{4,3},{5,4},{6,5},{7,6},{8,7},{9,8},{10,9},{11,1... | collective-permute-start | bytes 1572872 | tf_op jit(solution)/shard_map/ppermute | solution.py:20
  9.8 89.6 %all-to-all-start.2 = ((s32[32,1,8]{2,1,0:T(1,128)}), s32[32,1,8]{2,1,0:T(1,128)S(1)}, u32[]{:S(2)}, u32[]{:S(2)}) async-start(s32[32,1,8]{2,1,0:T(1,128)} %bitcast.21), calls=%async_computation.2 | async-start | bytes 32768 | tf_op jit(solution)/shard_map/all_to_all | solution.py:112
  29.0 9.9 %copy-start.2 = (f32[3,128,64]{1,2,0:T(8,128)S(1)}, f32[3,128,64]{1,2,0:T(8,128)}, u32[]{:S(2)}) copy-start(f32[3,128,64]{1,2,0:T(8,128)} %param.27) | copy-start | bytes 294916
  29.0 9.9 %copy-start.1 = (f32[128,64,64]{0,2,1:T(8,128)S(1)}, f32[128,64,64]{0,2,1:T(8,128)}, u32[]{:S(2)}) copy-start(f32[128,64,64]{0,2,1:T(8,128)} %param.25) | copy-start | bytes 6291460
  38.6 1.7 copy-start.7
  38.9 51.2 %copy-start.8 = (s32[128,6]{0,1:T(8,128)S(1)}, s32[128,6]{0,1:T(8,128)}, u32[]{:S(2)}) copy-start(s32[128,6]{0,1:T(8,128)} %param.30) | copy-start | bytes 9220
  38.9 51.3 %copy-start.3 = (f32[3,16,64]{2,1,0:T(8,128)S(1)}, f32[3,16,64]{2,1,0:T(8,128)}, u32[]{:S(2)}) copy-start(f32[3,16,64]{2,1,0:T(8,128)} %param.28) | copy-start | bytes 36868
  99.5 9.6 %all-to-all-start = ((s32[32,1,64]{2,1,0:T(1,128)}), s32[32,1,64]{2,1,0:T(1,128)S(1)}, u32[]{:S(2)}, u32[]{:S(2)}) async-start(s32[32,1,64]{2,1,0:T(1,128)} %all_to_all.26), calls=%async_computation | async-start | bytes 32768 | tf_op jit(solution)/shard_map/all_to_all | solution.py:112
  109.1 14.5 %all-to-all-start.3 = ((f32[32,8,256]{2,1,0:T(8,128)}), f32[32,8,256]{2,1,0:T(8,128)S(1)}, u32[]{:S(2)}, u32[]{:S(2)}) async-start(f32[32,8,256]{2,1,0:T(8,128)} %bitcast_select_fusion), calls=%async_computation.3 | async-start | bytes 524288 | tf_op jit(solution)/shard_map/all_to_all | solution.py:115
  123.7 180.8 %all-to-all-start.1 = ((f32[32,64,256]{2,1,0:T(8,128)}), f32[32,64,256]{2,1,0:T(8,128)}, u32[]{:S(2)}, u32[]{:S(2)}) async-start(f32[32,64,256]{2,1,0:T(8,128)} %broadcast_select_fusion.2), calls=%async_computation.1 | async-start | bytes 4194304 | tf_op jit(solution)/shard_map/all_to_all | solution.py:115
  145.2 1.5 copy-start.5
where the time goes:
time: 344 us; the launch traced here: 343 us
  other arithmetic  187 us (54%)
  local copies, waits for them, and re-layouts  61.4 us (18%)
  blocking collectives  41.9 us (12%)
  starting transfers between devices  24.1 us (7%)
  matrix products  17.5 us (5%)
  loops' own time  5.56 us (2%)
  waiting for transfers between devices  5.25 us (2%)
    reduce_sum x24, other arithmetic, one_accumulate(): jnp.sum(values * nearby[:, None, 3 * width:], axis=2) * weight[:, None]  128 us
    all_gather x1, blocking collectives, local(): every_top = lax.all_gather(top_table, ('dom', 'sub'), axis=0, tiled=True)  41.9 us
    reduce_sum x48, other arithmetic, couple_accumulate(): jnp.sum(values * piece[:, None, 0:rank_width], axis=2) * weight[:, None]  31.9 us
    gather x24, local copies, waits for them, and re-layouts, one_accumulate(): nearby = jnp.take(table, chosen, axis=0)  14.8 us
    gather x3, local copies, waits for them, and re-layouts, fetch(): jnp.take(flattened, jnp.minimum(places, shards * capacity - 1), axis=0)  11.1 us
    all_to_all x2, starting transfers between devices, fetch(): lax.all_to_all(requests, ('dom', 'sub'), split_axis=0, concat_axis=0, til...  10.9 us
    another operation x4, other arithmetic  9.9 us
    dot_general x1, matrix products, local(): jnp.einsum('lrp,lp->lr', leaf_basis, charges, precision=highest)  9.66 us
  transfers between devices with their start and end apart: 6, of which 1 were waited for; matrix products, arithmetic and copies ran while one was open for 65% of the time, Pallas kernels for 0%

commit v1 on v0

v1 whole, which is shorter than its diff:
```python
import functools

import jax
import jax.numpy as jnp
from jax import lax
from jax.experimental import pallas as pl
from jax.experimental.pallas import tpu as pltpu
from jax.sharding import PartitionSpec as P

soften = 0.25
axes = ("dom", "sub")
highest = lax.Precision.HIGHEST


def split(value):
    high = value.astype(jnp.bfloat16).astype(jnp.float32)
    rest = value - high
    middle = rest.astype(jnp.bfloat16).astype(jnp.float32)
    return high, middle, rest - middle


def stack_rows(rows, width):
    place = lax.broadcasted_iota(jnp.int32, (8, width), 0)
    block = jnp.zeros((8, width), jnp.float32)
    for index, row in enumerate(rows):
        block = jnp.where(place == index, row, block)
    return block


def target_side(x, y, z):
    norm = x * x + y * y + z * z + soften
    block = stack_rows((-2.0 * x, -2.0 * y, -2.0 * z, 1.0, norm), x.shape[1])
    high, middle, low = split(block)
    joined = jnp.concatenate([high, high, middle, high, low, middle], axis=0)
    return joined.T.astype(jnp.bfloat16)


def source_side(x, y, z):
    norm = x * x + y * y + z * z
    block = stack_rows((x, y, z, norm, 1.0), x.shape[1])
    high, middle, low = split(block)
    return jnp.concatenate([high, middle, high, low, high, middle], axis=0).astype(jnp.bfloat16)


def near_kernel(entries, first, picks, table, out):
    width = out.shape[1]

    def parts(index):
        row = table[pl.ds(index, 1), :]
        return tuple(row[:, c * width : (c + 1) * width] for c in range(4))

    def one_row(row, carry):
        x, y, z, _ = parts(first + row)
        left = target_side(x, y, z)
        total = jnp.zeros((width, 128), jnp.float32)
        for column in range(entries):
            x, y, z, charge = parts(picks[row * entries + column])
            squares = jnp.dot(left, source_side(x, y, z), preferred_element_type=jnp.float32)
            terms = lax.rsqrt(squares) * charge
            for start in range(0, width, 128):
                total += terms[:, start : start + 128]
        out[pl.ds(row, 1), :] = jnp.sum(total.T, axis=0, keepdims=True)
        return carry

    lax.fori_loop(0, out.shape[0], one_row, 0, unroll=2)


def near_field(picks, table, rows, width, first):
    entries = picks.shape[1]
    return pl.pallas_call(
        functools.partial(near_kernel, entries, first),
        out_shape=jax.ShapeDtypeStruct((rows, width), jnp.float32),
        in_specs=[
            pl.BlockSpec(memory_space=pltpu.SMEM),
            pl.BlockSpec(memory_space=pltpu.VMEM),
        ],
        out_specs=pl.BlockSpec(memory_space=pltpu.VMEM),
        compiler_params=pltpu.CompilerParams(vmem_limit_bytes=32 * 1024 * 1024),
        cost_estimate=pl.CostEstimate(
            flops=rows * entries * width * width * 100,
            bytes_accessed=table.size * 4,
            transcendentals=rows * entries * width * width,
        ),
        name="near",
    )(picks.reshape(-1), table)


def far_kernel(entries, picks, own, table, out):
    rank = out.shape[1]
    lane = lax.broadcasted_iota(jnp.int32, (1, 128), 1)

    def halves(ref, index):
        row = ref[pl.ds(index, 1), :]
        first, second = row[:, :128], row[:, 128:]
        return first, second, pltpu.roll(first, 64, 1), pltpu.roll(second, 64, 1)

    def one_row(row, carry):
        first, second, turned, _ = halves(own, row)
        left = target_side(first, turned, second)[:rank]
        total = jnp.zeros((rank, 128), jnp.float32)
        for pair in range(0, entries, 2):
            a0, a1, a2, a3 = halves(table, picks[row * entries + pair])
            b0, b1, b2, b3 = halves(table, picks[row * entries + pair + 1])
            x = jnp.where(lane < 64, a0, b2)
            y = jnp.where(lane < 64, a2, b0)
            z = jnp.where(lane < 64, a1, b3)
            moment = jnp.where(lane < 64, a3, b1)
            squares = jnp.dot(left, source_side(x, y, z), preferred_element_type=jnp.float32)
            total += lax.rsqrt(squares) * moment
        out[pl.ds(row, 1), :] = jnp.sum(total.T, axis=0, keepdims=True)
        return carry

    lax.fori_loop(0, out.shape[0], one_row, 0, unroll=2)


def far_field(picks, own, table, rows, rank):
    entries = picks.shape[1]
    return pl.pallas_call(
        functools.partial(far_kernel, entries),
        out_shape=jax.ShapeDtypeStruct((rows, rank), jnp.float32),
        in_specs=[
            pl.BlockSpec(memory_space=pltpu.SMEM),
            pl.BlockSpec(memory_space=pltpu.VMEM),
            pl.BlockSpec(memory_space=pltpu.VMEM),
        ],
        out_specs=pl.BlockSpec(memory_space=pltpu.VMEM),
        compiler_params=pltpu.CompilerParams(vmem_limit_bytes=48 * 1024 * 1024),
        cost_estimate=pl.CostEstimate(
            flops=rows * entries * rank * rank * 100,
            bytes_accessed=table.size * 4,
            transcendentals=rows * entries * rank * rank,
        ),
        name="far",
    )(picks.reshape(-1), own, table)


def make_table(moments, nodes):
    return jnp.concatenate([nodes[0], nodes[1], nodes[2], moments], axis=1)


def local(
    charges,
    points,
    leaf_basis,
    child_transfer,
    parent_transfer,
    nodes_leaf,
    nodes_mid,
    nodes_top,
    near_list,
    far_leaf,
    far_mid,
    far_top,
):
    shards = lax.axis_size(axes)
    leaf_count, width = charges.shape
    mid_count = leaf_count // 8
    top_count = mid_count // 8
    rank = leaf_basis.shape[1]

    own_points = jnp.concatenate([points[0], points[1], points[2], charges], axis=1)
    before = lax.ppermute(own_points, axes, [(i, i + 1) for i in range(shards - 1)])
    after = lax.ppermute(own_points, axes, [(i + 1, i) for i in range(shards - 1)])

    leaf_moments = jnp.einsum("lrp,lp->lr", leaf_basis, charges, precision=highest)
    mid_moments = (
        jnp.einsum("lij,lj->li", child_transfer, leaf_moments, precision=highest)
        .reshape(mid_count, 8, rank)
        .sum(axis=1)
    )
    top_moments = (
        jnp.einsum("lij,lj->li", parent_transfer, mid_moments, precision=highest)
        .reshape(top_count, 8, rank)
        .sum(axis=1)
    )
    count = leaf_count + mid_count + top_count
    padded = -(-(count + 1) // 8) * 8
    own = jnp.concatenate(
        [
            make_table(leaf_moments, nodes_leaf),
            make_table(mid_moments, nodes_mid),
            make_table(top_moments, nodes_top),
            jnp.zeros((padded - count, 4 * rank), jnp.float32),
        ],
        axis=0,
    )
    every = lax.all_gather(own, axes, axis=0, tiled=True)

    def rows_of(lists, per_shard, offset):
        row = lists // per_shard * padded + offset + lists % per_shard
        return jnp.where(lists >= 0, row, count)

    far_picks = jnp.concatenate(
        [
            rows_of(far_leaf, leaf_count, 0),
            rows_of(far_mid, mid_count, leaf_count),
            rows_of(far_top, top_count, leaf_count + mid_count),
        ],
        axis=0,
    )

    position = lax.axis_index(axes)
    near_table = jnp.concatenate(
        [before, own_points, after, jnp.zeros((8, 4 * width), jnp.float32)], axis=0
    )
    near_picks = jnp.where(
        near_list >= 0, near_list - (position - 1) * leaf_count, 3 * leaf_count
    )
    near_sum = near_field(near_picks, near_table, leaf_count, width, leaf_count)

    far = far_field(far_picks, own, every, count, rank)
    leaf_local = far[:leaf_count]
    mid_local = far[leaf_count : leaf_count + mid_count]
    top_local = far[leaf_count + mid_count :]
    mid_down = mid_local + jnp.einsum(
        "lji,lj->li", parent_transfer, jnp.repeat(top_local, 8, axis=0), precision=highest
    )
    leaf_down = leaf_local + jnp.einsum(
        "lji,lj->li", child_transfer, jnp.repeat(mid_down, 8, axis=0), precision=highest
    )
    return jnp.einsum("lrp,lr->lp", leaf_basis, leaf_down, precision=highest) + near_sum


def solution(mesh):
    row = P(axes, None)
    plane = P(None, axes, None)
    stack = P(axes, None, None)
    return jax.shard_map(
        local,
        mesh=mesh,
        in_specs=(row, plane, stack, stack, stack, plane, plane, plane, row, row, row, row),
        out_specs=row,
        check_vma=False,
    )
```

time: 344 us -> 155 us (0.45)
  other arithmetic: 187 us -> 1.9 us
  Pallas kernels: 0 us -> 82.2 us
  local copies, waits for them, and re-layouts: 61.4 us -> 9.19 us
  blocking collectives: 41.9 us -> 0 us
  starting transfers between devices: 24.1 us -> 3.86 us
  between operations: 0.64 us -> 13.8 us
  waiting for transfers between devices: 5.25 us -> 16.4 us
  matrix products: 17.5 us -> 27.8 us
  loops' own time: 5.56 us -> 0 us
    reduce_sum x74 -> x0, other arithmetic: 160 us -> none  [the longest x24 128 us: one_accumulate(): jnp.sum(values * nearby[:, None, 3 * width:], axis=2) * weight[:, None]]
    pallas_call x0 -> x2, Pallas kernels: none -> 82.2 us  [the longest x1 47.3 us: near_field(): pl.pallas_call(functools.partial(near_kernel, entries, first), out_shape=...]
    all_gather x1 -> x0, blocking collectives: 41.9 us -> none  [local(): every_top = lax.all_gather(top_table, ('dom', 'sub'), axis=0, tiled=True)]
    gather x30 -> x0, local copies, waits for them, and re-layouts: 36 us -> none  [the longest x24 14.8 us: one_accumulate(): nearby = jnp.take(table, chosen, axis=0)]
    all_to_all x4 -> x0, starting transfers between devices: 19.6 us -> none  [the longest x2 10.9 us: fetch(): lax.all_to_all(requests, ('dom', 'sub'), split_axis=0, concat_axis=0, til...]
    all_gather x0 -> x1, waiting for transfers between devices: none -> 12.8 us  [local(): every = lax.all_gather(own, axes, axis=0, tiled=True)]
    dot_general x0 -> x2, matrix products: none -> 10.3 us  [the longest x1 6.6 us: local(): jnp.einsum('lij,lj->li', child_transfer, leaf_moments, precision=highest)]
    another operation x4 -> x0, other arithmetic: 9.9 us -> none
  transfers between devices with their start and end apart: 6 -> 3, of which waited for: 1 -> 2; matrix products, arithmetic and copies ran while one was open for 65% -> 1% of each run, Pallas kernels for 0% -> 30%
where the time goes in v1:
time: 155 us
  Pallas kernels  82.2 us (53%)
  matrix products  27.8 us (18%)
  waiting for transfers between devices  16.4 us (11%)
  between operations  13.8 us (9%)
  local copies, waits for them, and re-layouts  9.19 us (6%)
  starting transfers between devices  3.86 us (2%)
  other arithmetic  1.9 us (1%)
    pallas_call x1, Pallas kernels, near_field(): pl.pallas_call(functools.partial(near_kernel, entries, first), out_shape=...  47.3 us
    pallas_call x1, Pallas kernels, far_field(): pl.pallas_call(functools.partial(far_kernel, entries), out_shape=jax.Shap...  34.9 us
    all_gather x1, waiting for transfers between devices, local(): every = lax.all_gather(own, axes, axis=0, tiled=True)  12.8 us
    dot_general x1, matrix products, local(): jnp.einsum('lrp,lp->lr', leaf_basis, charges, precision=highest)  9.67 us
    unnamed x32, local copies, waits for them, and re-layouts  8.45 us
    dot_general x1, matrix products, local(): jnp.einsum('lij,lj->li', child_transfer, leaf_moments, precision=highest)  6.6 us
    dot_general x1, matrix products, local(): jnp.einsum('lrp,lr->lp', leaf_basis, leaf_down, precision=highest)  6.44 us
    dot_general x1, matrix products, local(): jnp.einsum('lji,lj->li', child_transfer, jnp.repeat(mid_down, 8, axis=0),...  3.68 us
  transfers between devices with their start and end apart: 3, of which 2 were waited for; matrix products, arithmetic and copies ran while one was open for 1% of the time, Pallas kernels for 30%

profile of v1, /device:TPU:0, one launch (start us, length us, event | category | flops | bytes accessed | tf_op | source)
XLA Modules:
  0.0 155.1 jit_solution(11776821464569391153)
XLA Ops:
  6.5 0.0 copy-start
  6.5 0.0 all-gather.2.cloned.1.call-start
  6.5 5.7 %copy.42 = f32[128,64,64]{2,1,0:T(8,128)} copy(f32[128,64,64]{0,2,1:T(8,128)} %param.15) | data formatting | bytes 4194304 | tf_op args[3]
  12.2 0.0 copy-done.5
  12.2 9.7 %fusion = f32[128,1,64]{2,1,0:T(1,128)S(1)} fusion(f32[128,64,256]{2,1,0:T(8,128)} %param.14, f32[128,256,1]{1,0,2:T(8,128)S(1)} %bitcast.73), kind=kOutput, calls=%fused_computation.4 | convolution fusion | flops 25165824 | bytes 8552448 | tf_op jit(solution)/shard_map/lrp,lp->lr/dot_general | solution.py:165
  21.9 0.0 copy-done.3
  21.9 0.0 copy-start.7
  21.9 0.0 copy-start.8
  21.9 0.0 copy-start.12
  22.0 0.0 copy-start.6
  22.0 0.0 copy-start.9
  22.0 0.0 copy-start.13
  22.0 0.0 copy-start.10
  22.0 0.0 copy-start.11
  22.0 6.6 %fusion.2 = f32[128,1,64]{2,1,0:T(1,128)S(1)} fusion(f32[128,64,64]{2,1,0:T(8,128)S(1)} %copy-done.3, f32[128,1,64]{2,1,0:T(1,128)S(1)} %fusion), kind=kOutput, calls=%fused_computation.11 | convolution fusion | flops 6291456 | bytes 2162688 | tf_op jit(solution)/shard_map/lij,lj->li/dot_general | solution.py:167
  28.7 0.0 copy-done
  28.7 0.9 fusion.21
  29.6 0.0 copy-done.7
  29.6 0.1 copy.46
  29.7 0.1 copy.47
  29.8 0.1 copy.48
  29.9 0.0 copy-done.8
  30.0 0.0 copy-done.12
  30.0 0.1 pad.23.clone
  30.1 0.8 maximum_maximum_fusion.1.own
  30.9 0.0 all-gather.2.cloned.1.call-update
  30.9 0.0 copy-done.6
  31.0 2.4 %collective-permute-start = (f32[128,1024]{1,0:T(8,128)S(1)}, f32[128,1024]{1,0:T(8,128)S(1)}, u32[]{:S(2)}, u32[]{:S(2)}) collective-permute-start(f32[128,1024]{1,0:T(8,128)S(1)} %pad_maximum_fusion), channel_id=1, source_target_pairs={{0,1},{1,2},{2,3},{3,4},{4,5},{5,6},{6,7},{7,8},{8,9},{9,10},{10,1... | collective-permute-start | bytes 1572872 | tf_op jit(solution)/shard_map/ppermute | solution.py:162
  33.4 1.5 collective-permute-start.1
  34.9 0.1 copy.25
  35.0 0.1 copy.26
  35.1 0.0 copy-done.10
  35.1 0.1 pad_add_fusion
  35.2 0.1 copy.27
  35.3 0.1 reshape.18.picks
  35.5 0.1 copy.31
  35.6 0.1 reshape.23.picks
  35.7 0.0 collective-permute-done
  35.7 3.6 %collective-permute-done.1 = f32[128,1024]{1,0:T(8,128)S(1)} collective-permute-done((f32[128,1024]{1,0:T(8,128)S(1)}, f32[128,1024]{1,0:T(8,128)S(1)}, u32[]{:S(2)}, u32[]{:S(2)}) %collective-permute-start.1) | collective-permute-done | bytes 524320 | tf_op jit(solution)/shard_map/ppermute | solution.py:163
  39.3 0.2 maximum_maximum_fusion.table
  39.5 47.3 %near.1 = f32[128,256]{1,0:T(8,128)S(1)} custom-call(s32[768]{0:T(1024)S(1)} %reshape.23.picks, f32[392,1024]{1,0:T(8,128)S(1)} %maximum_maximum_fusion.table), custom_call_target="tpu_custom_call" | custom-call | flops 5033164800 | bytes 1605632 | tf_op jit(solution)/shard_map/near/pallas_call | solution.py:70
  86.7 12.8 %all-gather.2.cloned.1.call-done.table = f32[4864,256]{1,0:T(8,128)} async-done(((f32[152,256]{1,0:T(8,128)}), f32[4864,256]{1,0:T(8,128)}) %all-gather.2.cloned.1.call-update) | async-done | bytes 4980752 | tf_op jit(solution)/shard_map/all_gather | solution.py:187
  99.6 2.4 %copy-done.2 = f32[4864,256]{1,0:T(8,128)S(1)} copy-done((f32[4864,256]{1,0:T(8,128)S(1)}, f32[4864,256]{1,0:T(8,128)}, u32[]{:S(2)}) %copy-start.2) | copy-done | bytes 4980760
  102.0 34.9 %far.1 = f32[146,64]{1,0:T(8,128)S(1)} custom-call(s32[2336]{0:T(1024)S(1)} %reshape.18.picks, f32[152,256]{1,0:T(8,128)S(1)} %copy-done.1, f32[4864,256]{1,0:T(8,128)S(1)} %copy-done.2), custom_call_target="tpu_custom_call" | custom-call | flops 956825600 | bytes 4980736 | tf_op jit(solution)/shard_map/far/pallas_call | solution.py:118
  136.9 0.5 fusion.22
  137.5 3.7 %fusion.23 = f32[128,1,64]{2,1,0:T(1,128)S(1)} fusion(f32[128,64,1]{1,2,0:T(1,128)S(1)} %bitcast.77, f32[128,64,64]{2,1,0:T(8,128)S(1)} %copy-done.4), kind=kOutput, calls=%fused_computation.60 | convolution fusion | flops 6291456 | bytes 2162688 | tf_op jit(solution)/shard_map/lji,lj->li/dot_general | solution.py:218
  141.2 6.4 %fusion.24 = f32[128,1,256]{2,1,0:T(1,128)S(1)} fusion(f32[128,64,1]{1,2,0:T(1,128)S(1)} %bitcast.76, f32[128,64,256]{2,1,0:T(8,128)} %param.14), kind=kOutput, calls=%fused_computation.61 | convolution fusion | flops 25165824 | bytes 8552448 | tf_op jit(solution)/shard_map/lrp,lr->lp/dot_general | solution.py:221
  147.6 0.7 bitcast_add_fusion
  (29 shorter events, 0.3 us)
Async XLA Ops:
  6.5 22.1 %copy-start = (f32[16,64,64]{2,1,0:T(8,128)S(1)}, f32[16,64,64]{2,1,0:T(8,128)}, u32[]{:S(2)}) copy-start(f32[16,64,64]{2,1,0:T(8,128)} %param.16) | copy-start | bytes 786436
  6.5 5.7 %copy-start.5 = (f32[128,256]{1,0:T(8,128)S(1)}, f32[128,256]{1,0:T(8,128)}, u32[]{:S(2)}) copy-start(f32[128,256]{1,0:T(8,128)} %param.12) | copy-start | bytes 393220
  6.5 93.0 %all-gather.2.cloned.1.call-start = ((), (), s32[]{:S(2)}) async-start(), calls=%async_computation | async-start | bytes 5136384 | tf_op jit(solution)/shard_map/all_gather | solution.py:187
  12.2 9.7 %copy-start.3 = (f32[128,64,64]{2,1,0:T(8,128)S(1)}, f32[128,64,64]{2,1,0:T(8,128)}, u32[]{:S(2)}) copy-start(f32[128,64,64]{2,1,0:T(8,128)} %copy.42) | copy-start | bytes 6291460
  21.9 7.7 %copy-start.7 = (f32[3,128,64]{1,2,0:T(8,128)S(1)}, f32[3,128,64]{1,2,0:T(8,128)}, u32[]{:S(2)}) copy-start(f32[3,128,64]{1,2,0:T(8,128)} %param.17) | copy-start | bytes 294916
  21.9 8.0 %copy-start.8 = (f32[3,16,64]{2,1,0:T(8,128)S(1)}, f32[3,16,64]{2,1,0:T(8,128)}, u32[]{:S(2)}) copy-start(f32[3,16,64]{2,1,0:T(8,128)} %param.18) | copy-start | bytes 36868
  21.9 8.0 %copy-start.12 = (f32[3,2,64]{2,1,0:T(2,128)S(1)}, f32[3,2,64]{2,1,0:T(2,128)}, u32[]{:S(2)}) copy-start(f32[3,2,64]{2,1,0:T(2,128)} %param.19) | copy-start | bytes 4612
  22.0 9.0 %copy-start.6 = (f32[3,128,256]{2,1,0:T(8,128)S(1)}, f32[3,128,256]{2,1,0:T(8,128)}, u32[]{:S(2)}) copy-start(f32[3,128,256]{2,1,0:T(8,128)} %param.13) | copy-start | bytes 1179652
  22.0 12.9 %copy-start.9 = (s32[16,16]{1,0:T(8,128)S(1)}, s32[16,16]{1,0:T(8,128)}, u32[]{:S(2)}) copy-start(s32[16,16]{1,0:T(8,128)} %param.22) | copy-start | bytes 3076
  22.0 13.0 %copy-start.13 = (s32[2,16]{1,0:T(2,128)S(1)}, s32[2,16]{1,0:T(2,128)}, u32[]{:S(2)}) copy-start(s32[2,16]{1,0:T(2,128)} %param.23) | copy-start | bytes 388
  22.0 13.1 %copy-start.10 = (s32[128,16]{0,1:T(8,128)S(1)}, s32[128,16]{0,1:T(8,128)}, u32[]{:S(2)}) copy-start(s32[128,16]{0,1:T(8,128)} %param.21) | copy-start | bytes 24580
  22.0 13.4 %copy-start.11 = (s32[128,6]{0,1:T(8,128)S(1)}, s32[128,6]{0,1:T(8,128)}, u32[]{:S(2)}) copy-start(s32[128,6]{0,1:T(8,128)} %param.20) | copy-start | bytes 9220
  31.0 4.7 %collective-permute-start = (f32[128,1024]{1,0:T(8,128)S(1)}, f32[128,1024]{1,0:T(8,128)S(1)}, u32[]{:S(2)}, u32[]{:S(2)}) collective-permute-start(f32[128,1024]{1,0:T(8,128)S(1)} %pad_maximum_fusion), channel_id=1, source_target_pairs={{0,1},{1,2},{2,3},{3,4},{4,5},{5,6},{6,7},{7,8},{8,9},{9,10},{10,1... | collective-permute-start | bytes 1572872 | tf_op jit(solution)/shard_map/ppermute | solution.py:162
  33.4 5.9 %collective-permute-start.1 = (f32[128,1024]{1,0:T(8,128)S(1)}, f32[128,1024]{1,0:T(8,128)S(1)}, u32[]{:S(2)}, u32[]{:S(2)}) collective-permute-start(f32[128,1024]{1,0:T(8,128)S(1)} %pad_maximum_fusion), channel_id=1, source_target_pairs={{1,0},{2,1},{3,2},{4,3},{5,4},{6,5},{7,6},{8,7},{9,8},{10,9},{11,1... | collective-permute-start | bytes 1572872 | tf_op jit(solution)/shard_map/ppermute | solution.py:163
  39.5 60.1 %copy-start.1 = (f32[152,256]{1,0:T(8,128)S(1)}, f32[152,256]{1,0:T(8,128)}, u32[]{:S(2)}) copy-start(f32[152,256]{1,0:T(8,128)} %maximum_maximum_fusion.1.own) | copy-start | bytes 466948
  99.6 2.4 %copy-start.2 = (f32[4864,256]{1,0:T(8,128)S(1)}, f32[4864,256]{1,0:T(8,128)}, u32[]{:S(2)}) copy-start(f32[4864,256]{1,0:T(8,128)} %all-gather.2.cloned.1.call-done.table) | copy-start | bytes 14942212
  102.0 35.5 %copy-start.4 = (f32[128,64,64]{2,1,0:T(8,128)S(1)}, f32[128,64,64]{2,1,0:T(8,128)}, u32[]{:S(2)}) copy-start(f32[128,64,64]{2,1,0:T(8,128)} %copy.42) | copy-start | bytes 6291460
Sparse Core Ops, SparseCore 0:
  31.0 68.4 all-gather.1

commit v2 on v1

--- a/solution.py
+++ b/solution.py
@@ -9,7 +9,6 @@
 
 soften = 0.25
 axes = ("dom", "sub")
-highest = lax.Precision.HIGHEST
 
 
 def split(value):
@@ -62,7 +61,7 @@
         out[pl.ds(row, 1), :] = jnp.sum(total.T, axis=0, keepdims=True)
         return carry
 
-    lax.fori_loop(0, out.shape[0], one_row, 0, unroll=2)
+    lax.fori_loop(0, out.shape[0], one_row, 0, unroll=8)
 
 
 def near_field(picks, table, rows, width, first):
@@ -85,57 +84,86 @@
     )(picks.reshape(-1), table)
 
 
-def far_kernel(entries, picks, own, table, out):
+def far_kernel(entries, picks, own_xy, own_zm, table_xy, table_zm, out, near_xy, near_zm):
     rank = out.shape[1]
-    lane = lax.broadcasted_iota(jnp.int32, (1, 128), 1)
-
-    def halves(ref, index):
-        row = ref[pl.ds(index, 1), :]
-        first, second = row[:, :128], row[:, 128:]
-        return first, second, pltpu.roll(first, 64, 1), pltpu.roll(second, 64, 1)
-
-    def one_row(row, carry):
-        first, second, turned, _ = halves(own, row)
-        left = target_side(first, turned, second)[:rank]
+    half = entries // 2
+    lower = lax.broadcasted_iota(jnp.int32, (half, 128), 1) < 64
+    slot = lax.rem(lax.broadcasted_iota(jnp.int32, (rank, 15 * half), 1), half)
+
+    def spread(row):
+        return jnp.broadcast_to(row, (half, 128))
+
+    def one_row(row, buffer):
+        for e in range(entries):
+            pick = picks[row * entries + e]
+            near_xy[buffer, pl.ds(e, 1), :] = table_xy[pl.ds(pick, 1), :]
+            near_zm[buffer, pl.ds(e, 1), :] = table_zm[pl.ds(pick, 1), :]
+        xy = spread(own_xy[pl.ds(row, 1), :])
+        zm = spread(own_zm[pl.ds(row, 1), :])
+        yx = pltpu.roll(xy, 64, 1)
+        ones = jnp.ones((half, 128), jnp.float32)
+        left = []
+        for value in (xy, yx, zm):
+            h, m, _ = split(-2.0 * value)
+            left += [h, h, m]
+        left += list(split(xy * xy + yx * yx + zm * zm + soften)) + [ones, ones, ones]
+        left = jnp.concatenate(left, axis=0)[:, :rank].T
+        a, b = near_xy[buffer, :half, :], near_xy[buffer, half:, :]
+        c, d = near_zm[buffer, :half, :], near_zm[buffer, half:, :]
+        x = jnp.where(lower, a, pltpu.roll(b, 64, 1))
+        y = jnp.where(lower, pltpu.roll(a, 64, 1), b)
+        z = jnp.where(lower, c, pltpu.roll(d, 64, 1))
+        moment = jnp.where(lower, pltpu.roll(c, 64, 1), d)
+        right = []
+        for value in (x, y, z):
+            h, m, _ = split(value)
+            right += [h, m, h]
+        right += [ones, ones, ones] + list(split(x * x + y * y + z * z))
+        right = jnp.concatenate(right, axis=0).astype(jnp.bfloat16)
         total = jnp.zeros((rank, 128), jnp.float32)
-        for pair in range(0, entries, 2):
-            a0, a1, a2, a3 = halves(table, picks[row * entries + pair])
-            b0, b1, b2, b3 = halves(table, picks[row * entries + pair + 1])
-            x = jnp.where(lane < 64, a0, b2)
-            y = jnp.where(lane < 64, a2, b0)
-            z = jnp.where(lane < 64, a1, b3)
-            moment = jnp.where(lane < 64, a3, b1)
-            squares = jnp.dot(left, source_side(x, y, z), preferred_element_type=jnp.float32)
-            total += lax.rsqrt(squares) * moment
+        chosen = jnp.concatenate([jnp.where(slot == e, left, 0.0) for e in range(half)], axis=0)
+        squares = jnp.dot(
+            chosen.astype(jnp.bfloat16), right, preferred_element_type=jnp.float32
+        )
+        for e in range(half):
+            total += lax.rsqrt(squares[e * rank : (e + 1) * rank]) * moment[e : e + 1, :]
         out[pl.ds(row, 1), :] = jnp.sum(total.T, axis=0, keepdims=True)
+
+    unroll = near_xy.shape[0]
+
+    def some_rows(step, carry):
+        for buffer in range(unroll):
+            one_row(step * unroll + buffer, buffer)
         return carry
 
-    lax.fori_loop(0, out.shape[0], one_row, 0, unroll=2)
-
-
-def far_field(picks, own, table, rows, rank):
-    entries = picks.shape[1]
+    lax.fori_loop(0, out.shape[0] // unroll, some_rows, 0)
+
+
+def far_field(picks, own_xy, own_zm, table_xy, table_zm, rank):
+    rows, entries = picks.shape
     return pl.pallas_call(
         functools.partial(far_kernel, entries),
         out_shape=jax.ShapeDtypeStruct((rows, rank), jnp.float32),
-        in_specs=[
-            pl.BlockSpec(memory_space=pltpu.SMEM),
-            pl.BlockSpec(memory_space=pltpu.VMEM),
-            pl.BlockSpec(memory_space=pltpu.VMEM),
-        ],
+        in_specs=[pl.BlockSpec(memory_space=pltpu.SMEM)]
+        + [pl.BlockSpec(memory_space=pltpu.VMEM)] * 4,
         out_specs=pl.BlockSpec(memory_space=pltpu.VMEM),
+        scratch_shapes=[pltpu.VMEM((8, entries, 128), jnp.float32)] * 2,
         compiler_params=pltpu.CompilerParams(vmem_limit_bytes=48 * 1024 * 1024),
         cost_estimate=pl.CostEstimate(
             flops=rows * entries * rank * rank * 100,
-            bytes_accessed=table.size * 4,
+            bytes_accessed=table_xy.size * 8,
             transcendentals=rows * entries * rank * rank,
         ),
         name="far",
-    )(picks.reshape(-1), own, table)
-
-
-def make_table(moments, nodes):
-    return jnp.concatenate([nodes[0], nodes[1], nodes[2], moments], axis=1)
+    )(picks.reshape(-1), own_xy, own_zm, table_xy, table_zm)
+
+
+def contract_last(matrices, vectors):
+    return jnp.sum(matrices * vectors[:, None, :], axis=2)
+
+
+def contract_first(matrices, vectors):
+    return jnp.sum(matrices * vectors[:, :, None], axis=1)
 
 
 def local(
@@ -158,33 +186,36 @@
     top_count = mid_count // 8
     rank = leaf_basis.shape[1]
 
+    count = leaf_count + mid_count + top_count
+    padded = -(-(count + 1) // 8) * 8
+    filler = jnp.zeros((padded - count, 2 * rank), jnp.float32)
+    nodes = (nodes_leaf, nodes_mid, nodes_top)
+
+    def joined(first, second):
+        return jnp.concatenate(
+            [jnp.concatenate(pair, axis=1) for pair in zip(first, second)] + [filler], axis=0
+        )
+
+    own_xy = joined([n[0] for n in nodes], [n[1] for n in nodes])
+    every_xy = lax.all_gather(own_xy, axes, axis=0, tiled=True)
+
     own_points = jnp.concatenate([points[0], points[1], points[2], charges], axis=1)
     before = lax.ppermute(own_points, axes, [(i, i + 1) for i in range(shards - 1)])
     after = lax.ppermute(own_points, axes, [(i + 1, i) for i in range(shards - 1)])
 
-    leaf_moments = jnp.einsum("lrp,lp->lr", leaf_basis, charges, precision=highest)
+    leaf_moments = contract_last(leaf_basis, charges)
     mid_moments = (
-        jnp.einsum("lij,lj->li", child_transfer, leaf_moments, precision=highest)
+        contract_last(child_transfer, leaf_moments)
         .reshape(mid_count, 8, rank)
         .sum(axis=1)
     )
     top_moments = (
-        jnp.einsum("lij,lj->li", parent_transfer, mid_moments, precision=highest)
+        contract_last(parent_transfer, mid_moments)
         .reshape(top_count, 8, rank)
         .sum(axis=1)
     )
-    count = leaf_count + mid_count + top_count
-    padded = -(-(count + 1) // 8) * 8
-    own = jnp.concatenate(
-        [
-            make_table(leaf_moments, nodes_leaf),
-            make_table(mid_moments, nodes_mid),
-            make_table(top_moments, nodes_top),
-            jnp.zeros((padded - count, 4 * rank), jnp.float32),
-        ],
-        axis=0,
-    )
-    every = lax.all_gather(own, axes, axis=0, tiled=True)
+    own_zm = joined([n[2] for n in nodes], (leaf_moments, mid_moments, top_moments))
+    every_zm = lax.all_gather(own_zm, axes, axis=0, tiled=True)
 
     def rows_of(lists, per_shard, offset):
         row = lists // per_shard * padded + offset + lists % per_shard
@@ -195,6 +226,7 @@
             rows_of(far_leaf, leaf_count, 0),
             rows_of(far_mid, mid_count, leaf_count),
             rows_of(far_top, top_count, leaf_count + mid_count),
+            jnp.full((padded - count, far_leaf.shape[1]), count, jnp.int32),
         ],
         axis=0,
     )
@@ -208,17 +240,13 @@
     )
     near_sum = near_field(near_picks, near_table, leaf_count, width, leaf_count)
 
-    far = far_field(far_picks, own, every, count, rank)
+    far = far_field(far_picks, own_xy, own_zm, every_xy, every_zm, rank)
     leaf_local = far[:leaf_count]
     mid_local = far[leaf_count : leaf_count + mid_count]
-    top_local = far[leaf_count + mid_count :]
-    mid_down = mid_local + jnp.einsum(
-        "lji,lj->li", parent_transfer, jnp.repeat(top_local, 8, axis=0), precision=highest
-    )
-    leaf_down = leaf_local + jnp.einsum(
-        "lji,lj->li", child_transfer, jnp.repeat(mid_down, 8, axis=0), precision=highest
-    )
-    return jnp.einsum("lrp,lr->lp", leaf_basis, leaf_down, precision=highest) + near_sum
+    top_local = far[leaf_count + mid_count : count]
+    mid_down = mid_local + contract_first(parent_transfer, jnp.repeat(top_local, 8, axis=0))
+    leaf_down = leaf_local + contract_first(child_transfer, jnp.repeat(mid_down, 8, axis=0))
+    return contract_first(leaf_basis, leaf_down) + near_sum
 
 
 def solution(mesh):

time: 155 us -> 169 us (1.090)
  waiting for transfers between devices: 16.4 us -> 80.7 us
  Pallas kernels: 82.2 us -> 48.9 us
  matrix products: 27.8 us -> 0 us
  other arithmetic: 1.9 us -> 15.1 us
  local copies, waits for them, and re-layouts: 9.19 us -> 5.27 us
    all_gather x1 -> x2, waiting for transfers between devices: 12.8 us -> 80 us  [the longest x1 59.3 us: local(): every_zm = lax.all_gather(own_zm, axes, axis=0, tiled=True)]
    dot_general x6 -> x0, matrix products: 27.8 us -> none  [the longest x1 9.67 us: local(): jnp.einsum('lrp,lp->lr', leaf_basis, charges, precision=highest)]
    pallas_call x1, Pallas kernels: 34.9 us -> 15.7 us  [far_field(): pl.pallas_call(functools.partial(far_kernel, entries), out_shape=jax.Shap...]
    pallas_call x1, Pallas kernels: 47.3 us -> 33.3 us  [near_field(): pl.pallas_call(functools.partial(near_kernel, entries, first), out_shape=...]
    reduce_sum x2 -> x8, other arithmetic: 0.05 us -> 9.84 us  [the longest x3 5.23 us: contract_last(): return jnp.sum(matrices * vectors[:, None, :], axis=2)]
    unnamed x32 -> x29, local copies, waits for them, and re-layouts: 8.45 us -> 4.15 us
    ppermute x1, waiting for transfers between devices: 3.58 us -> 0.01 us  [local(): lax.ppermute(own_points, axes, [(i + 1, i) for i in range(shards - 1)])]
  transfers between devices with their start and end apart: 3 -> 4, of which waited for: 2 -> 2; matrix products, arithmetic and copies ran while one was open for 1% -> 3% of each run, Pallas kernels for 30% -> 20%
where the time goes in v2:
time: 169 us
  waiting for transfers between devices  80.7 us (48%)
  Pallas kernels  48.9 us (29%)
  other arithmetic  15.1 us (9%)
  between operations  13.8 us (8%)
  local copies, waits for them, and re-layouts  5.27 us (3%)
  starting transfers between devices  5.17 us (3%)
    all_gather x1, waiting for transfers between devices, local(): every_zm = lax.all_gather(own_zm, axes, axis=0, tiled=True)  59.3 us
    pallas_call x1, Pallas kernels, near_field(): pl.pallas_call(functools.partial(near_kernel, entries, first), out_shape=...  33.3 us
    all_gather x1, waiting for transfers between devices, local(): every_xy = lax.all_gather(own_xy, axes, axis=0, tiled=True)  20.7 us
    pallas_call x1, Pallas kernels, far_field(): pl.pallas_call(functools.partial(far_kernel, entries), out_shape=jax.Shap...  15.7 us
    reduce_sum x3, other arithmetic, contract_last(): return jnp.sum(matrices * vectors[:, None, :], axis=2)  5.23 us
    reduce_sum x3, other arithmetic, contract_first(): return jnp.sum(matrices * vectors[:, :, None], axis=1)  4.57 us
    unnamed x29, local copies, waits for them, and re-layouts  4.15 us
    ppermute x1, starting transfers between devices, local(): lax.ppermute(own_points, axes, [(i, i + 1) for i in range(shards - 1)])  3.85 us
  transfers between devices with their start and end apart: 4, of which 2 were waited for; matrix products, arithmetic and copies ran while one was open for 3% of the time, Pallas kernels for 20%

profile of v2, /device:TPU:0, one launch (start us, length us, event | category | flops | bytes accessed | tf_op | source)
XLA Modules:
  0.0 168.9 jit_solution(9250920657860908194)
XLA Ops:
  6.5 4.7 %multiply_reduce_fusion.1 = f32[128,64]{1,0:T(8,128)S(1)} fusion(f32[128,64,256]{2,1,0:T(8,128)} %param.14, f32[128,256]{1,0:T(8,128)} %param.12), kind=kLoop, calls=%fused_computation.1 | loop fusion | flops 4186112 | bytes 8552448 | tf_op jit(solution)/shard_map/reduce_sum | solution.py:162
  11.2 0.0 copy-start.5
  11.2 0.0 copy-start.12
  11.3 0.0 copy-start.9
  11.3 0.0 copy-start.8
  11.3 0.0 copy-start.7
  11.3 0.1 copy.56
  11.4 0.0 copy-done.4
  11.4 0.3 multiply_reduce_fusion.3
  11.7 0.0 copy-start.10
  11.7 0.0 copy-start.11
  11.8 0.1 copy.57
  11.9 0.4 copy-done.5
  12.3 0.2 multiply_reduce_fusion.5
  12.6 0.1 copy.63
  12.7 0.1 copy.62
  12.8 0.1 copy.61
  12.9 0.1 pad.24.clone
  13.0 0.8 maximum_maximum_fusion.2
  13.8 0.0 all-gather.3.cloned.1.call-update
  13.8 0.0 all-gather.5.cloned.1.call-start
  13.8 0.7 all-gather.5.cloned.1.call-update
  14.6 0.9 pad_maximum_fusion
  15.5 1.3 collective-permute-start.1
  16.7 3.9 %collective-permute-start = (f32[128,1024]{1,0:T(8,128)}, f32[128,1024]{1,0:T(8,128)}, u32[]{:S(2)}, u32[]{:S(2)}) collective-permute-start(f32[128,1024]{1,0:T(8,128)} %pad_maximum_fusion), channel_id=1, source_target_pairs={{0,1},{1,2},{2,3},{3,4},{4,5},{5,6},{6,7},{7,8},{8,9},{9,10},{10,1... | collective-permute-start | bytes 1572872 | tf_op jit(solution)/shard_map/ppermute | solution.py:203
  20.6 0.7 compare_select_fusion
  21.3 0.1 copy.51
  21.4 0.1 copy.50
  21.5 0.1 pad.28.clone
  21.6 0.1 add_add_fusion
  21.7 0.1 copy.52
  21.8 0.1 reshape.18.picks
  21.9 0.7 subtract_select_fusion
  22.5 0.1 copy.60
  22.7 0.1 reshape.21.picks
  22.8 1.4 maximum_maximum_fusion.table
  24.2 33.3 %near.1 = f32[128,256]{1,0:T(8,128)S(1)} custom-call(s32[768]{0:T(1024)S(1)} %reshape.21.picks, f32[392,1024]{1,0:T(8,128)S(1)} %maximum_maximum_fusion.table), custom_call_target="tpu_custom_call" | custom-call | flops 5033164800 | bytes 1605632 | tf_op jit(solution)/shard_map/near/pallas_call | solution.py:69
  57.5 20.7 %all-gather.3.cloned.1.call-done.table_xy = f32[4864,128]{1,0:T(8,128)} async-done(((f32[152,128]{1,0:T(8,128)}), f32[4864,128]{1,0:T(8,128)}) %all-gather.3.cloned.1.call-update) | async-done | bytes 2490384 | tf_op jit(solution)/shard_map/all_gather | solution.py:200
  78.2 59.3 %all-gather.5.cloned.1.call-done.table_zm = f32[4864,128]{1,0:T(8,128)} async-done(((f32[152,128]{1,0:T(8,128)}), f32[4864,128]{1,0:T(8,128)}) %all-gather.5.cloned.1.call-update) | async-done | bytes 2490384 | tf_op jit(solution)/shard_map/all_gather | solution.py:218
  137.5 1.7 %copy-done.2 = f32[4864,128]{1,0:T(8,128)S(1)} copy-done((f32[4864,128]{1,0:T(8,128)S(1)}, f32[4864,128]{1,0:T(8,128)}, u32[]{:S(2)}) %copy-start.2) | copy-done | bytes 2490392
  139.2 1.7 %copy-done.3 = f32[4864,128]{1,0:T(8,128)S(1)} copy-done((f32[4864,128]{1,0:T(8,128)S(1)}, f32[4864,128]{1,0:T(8,128)}, u32[]{:S(2)}) %copy-start.3) | copy-done | bytes 2490392
  140.9 15.7 %far.1 = f32[152,64]{1,0:T(8,128)S(1)} custom-call(s32[2432]{0:T(1024)S(1)} %reshape.18.picks, f32[152,128]{1,0:T(8,128)S(1)} %copy-done.1, f32[152,128]{1,0:T(8,128)S(1)} %copy-done, f32[4864,128]{1,0:T(8,128)S(1)} %copy-done.2, f32[4864,128]{1,0:T(8,128)S(1)} %copy-done.3), custom_call_target="tpu_custom_call" | custom-call | flops 996147200 | bytes 4980736 | tf_op jit(solution)/shard_map/far/pallas_call | solution.py:144
  156.6 0.2 multiply_reduce_fusion.4
  156.9 0.1 copy.58
  156.9 0.2 multiply_reduce_fusion.2
  157.1 0.1 copy.59
  157.3 4.1 %multiply_reduce_fusion = f32[128,256]{1,0:T(8,128)S(1)} fusion(f32[128,64,256]{2,1,0:T(8,128)} %param.14, f32[128,64]{1,0:T(8,128)S(1)} %slice_add_fusion), kind=kLoop, calls=%fused_computation | loop fusion | flops 4161536 | bytes 8552448 | tf_op jit(solution)/shard_map/reduce_sum | solution.py:166
  161.4 0.7 add.68
  (35 shorter events, 0.2 us)
Async XLA Ops:
  6.5 4.8 %copy-start.4 = (f32[128,64,64]{0,2,1:T(8,128)S(1)}, f32[128,64,64]{0,2,1:T(8,128)}, u32[]{:S(2)}) copy-start(f32[128,64,64]{0,2,1:T(8,128)} %param.15) | copy-start | bytes 6291460
  6.5 71.6 %all-gather.3.cloned.1.call-start = ((), (), s32[]{:S(2)}) async-start(), calls=%async_computation | async-start | bytes 2568192 | tf_op jit(solution)/shard_map/all_gather | solution.py:200
  11.2 1.0 copy-start.5
  11.2 1.3 copy-start.12
  11.3 1.3 copy-start.9
  11.3 1.3 copy-start.8
  11.3 3.3 %copy-start.7 = (f32[3,128,256]{2,1,0:T(8,128)S(1)}, f32[3,128,256]{2,1,0:T(8,128)}, u32[]{:S(2)}) copy-start(f32[3,128,256]{2,1,0:T(8,128)} %param.13) | copy-start | bytes 1179652
  11.4 3.2 %copy-start.6 = (f32[128,256]{1,0:T(8,128)S(1)}, f32[128,256]{1,0:T(8,128)}, u32[]{:S(2)}) copy-start(f32[128,256]{1,0:T(8,128)} %param.12) | copy-start | bytes 393220
  11.7 8.9 %copy-start.10 = (s32[16,16]{1,0:T(8,128)S(1)}, s32[16,16]{1,0:T(8,128)}, u32[]{:S(2)}) copy-start(s32[16,16]{1,0:T(8,128)} %param.22) | copy-start | bytes 3076
  11.7 8.9 %copy-start.11 = (s32[128,16]{0,1:T(8,128)S(1)}, s32[128,16]{0,1:T(8,128)}, u32[]{:S(2)}) copy-start(s32[128,16]{0,1:T(8,128)} %param.21) | copy-start | bytes 24580
  13.8 123.7 %all-gather.5.cloned.1.call-start = ((), (), s32[]{:S(2)}) async-start(), calls=%async_computation.1 | async-start | bytes 2568192 | tf_op jit(solution)/shard_map/all_gather | solution.py:218
  15.5 7.4 %collective-permute-start.1 = (f32[128,1024]{1,0:T(8,128)}, f32[128,1024]{1,0:T(8,128)}, u32[]{:S(2)}, u32[]{:S(2)}) collective-permute-start(f32[128,1024]{1,0:T(8,128)} %pad_maximum_fusion), channel_id=1, source_target_pairs={{1,0},{2,1},{3,2},{4,3},{5,4},{6,5},{7,6},{8,7},{9,8},{10,9},{11,1... | collective-permute-start | bytes 1572872 | tf_op jit(solution)/shard_map/ppermute | solution.py:204
  16.7 6.1 %collective-permute-start = (f32[128,1024]{1,0:T(8,128)}, f32[128,1024]{1,0:T(8,128)}, u32[]{:S(2)}, u32[]{:S(2)}) collective-permute-start(f32[128,1024]{1,0:T(8,128)} %pad_maximum_fusion), channel_id=1, source_target_pairs={{0,1},{1,2},{2,3},{3,4},{4,5},{5,6},{6,7},{7,8},{8,9},{9,10},{10,1... | collective-permute-start | bytes 1572872 | tf_op jit(solution)/shard_map/ppermute | solution.py:203
  24.2 113.3 %copy-start = (f32[152,128]{1,0:T(8,128)S(1)}, f32[152,128]{1,0:T(8,128)}, u32[]{:S(2)}) copy-start(f32[152,128]{1,0:T(8,128)} %get-tuple-element.17.own_zm) | copy-start | bytes 233476
  24.2 113.3 %copy-start.1 = (f32[152,128]{1,0:T(8,128)S(1)}, f32[152,128]{1,0:T(8,128)}, u32[]{:S(2)}) copy-start(f32[152,128]{1,0:T(8,128)} %get-tuple-element.18.own_xy) | copy-start | bytes 233476
  137.5 1.7 %copy-start.2 = (f32[4864,128]{1,0:T(8,128)S(1)}, f32[4864,128]{1,0:T(8,128)}, u32[]{:S(2)}) copy-start(f32[4864,128]{1,0:T(8,128)} %all-gather.3.cloned.1.call-done.table_xy) | copy-start | bytes 7471108
  139.2 1.7 %copy-start.3 = (f32[4864,128]{1,0:T(8,128)S(1)}, f32[4864,128]{1,0:T(8,128)}, u32[]{:S(2)}) copy-start(f32[4864,128]{1,0:T(8,128)} %all-gather.5.cloned.1.call-done.table_zm) | copy-start | bytes 7471108
Sparse Core Ops, SparseCore 0:
  13.9 64.2 all-gather.2
  81.0 56.4 all-gather.4
